TPU v7x, 32 devices: a whole 2x2x4 slice. The times are simulated.
32 devices in a mesh: groups: 2 (over x), replica: 8 (over z, y), tensor: 2 (over core).
Axes of the slice: x: 2, y: 2, z: 4, core: 2. Of those that a mesh axis runs over, the one named last changes fastest.
Arguments:
- features: bfloat16 [768, 8192], P(('groups', 'replica'), 'tensor'), parts along dimension 0, may hold values from -6 to 6
- value_matrix: bfloat16 [8192, 512], P('tensor'), may hold values from -0.0625 to 0.0625
- adapter_down: bfloat16 [32, 16, 8192], P('replica', None, 'tensor'), may hold values from -0.0625 to 0.0625
- adapter_up: bfloat16 [32, 16, 512], P('replica', None, 'tensor'), may hold values from -0.75 to 0.75
- queries: bfloat16 [768, 4096], P(('groups', 'replica'), 'tensor'), parts along dimension 0, may hold values from -200 to 200
- new_key_rows: bfloat16 [768, 512], P(('groups', 'replica'), 'tensor'), parts along dimension 0, may hold values from -6 to 6
- stored_key_cache: bfloat16 [768, 128, 512], P(('groups', 'replica'), None, 'tensor'), parts along dimension 0, may hold values from -6 to 6
- stored_value_cache: bfloat16 [768, 128, 512], P(('groups', 'replica'), None, 'tensor'), parts along dimension 0, may hold values from -6 to 6
- cache_length: int32 [768], P(('groups', 'replica')), parts along dimension 0, may hold values from 2 to 128, as said below
- resident_adapter_index: int32 [384], P(('groups', 'replica')), parts along dimension 0, may hold values from 0 to 3
- panel_owner_slot: int32 [384], P(('groups', 'replica')), parts along dimension 0, may hold values from 0 to 15, as said below
- outgoing_rows: int32 [16, 8, 2], P(('groups', 'replica')), parts along dimension 0, may hold values from 0 to 3, as said below
- outgoing_counts: int32 [16, 8], P(('groups', 'replica')), parts along dimension 0, may hold values from 0 to 2, as said below
Outputs:
- new_value_rows: bfloat16 [768, 512], P(('groups', 'replica'), 'tensor'), parts along dimension 0
- attended: bfloat16 [768, 4096], P(('groups', 'replica'), 'tensor'), parts along dimension 0
There are 2 independent parts, one for each index of `groups`. A program takes and returns all parts, laid end to end along the dimension named above; an argument that names none is the same for every part. Nothing has to cross between parts.
Inputs may be any that keep to these rules, and one draw needn't show every extreme that they name: `cache_length`: each replica holds a request with 128 cached positions. For every new request, its slot panel_owner_slot % 2 is below the send count of the list of owner panel_owner_slot // 2 for the request's replica. The new requests of one replica take panels from exactly 8 distinct owners, 3 requests from each. The first outgoing_counts[o, h] entries of outgoing_rows[o, h] are distinct; later entries are arbitrary indices in range. `outgoing_counts`: every replica has a list with 2 live entries from some owner.
All inputs are finite; a program needn't handle non-finite values.
Results may differ from a plain program's by a relative error of at most 0.0051.
Values may be sent and summed in bfloat16 or wider, within the bound.
A program may use at most 128 MiB of HBM per device.

v0:
```python
import jax
import jax.numpy as jnp
from jax import lax
from jax.sharding import PartitionSpec as P

HD = 128
PANEL_SLOTS = 2
CTX = 128


ADAPTER_SCALE = 2.0


def attend(
    queries, new_key_rows, stored_key_cache, stored_value_cache, new_value_rows, cache_length
):
    row_count = queries.shape[0]
    kv_count = new_key_rows.shape[1] // HD
    group_size = queries.shape[1] // new_key_rows.shape[1]
    query_heads = queries.reshape(row_count, kv_count, group_size, HD)
    cached_keys = stored_key_cache.reshape(row_count, CTX, kv_count, HD)
    cached_values = stored_value_cache.reshape(row_count, CTX, kv_count, HD)
    fresh_keys = new_key_rows.reshape(row_count, kv_count, HD)
    fresh_values = new_value_rows.reshape(row_count, kv_count, HD)
    scale = 1.0 / jnp.sqrt(jnp.float32(HD))
    scores = (
        jnp.einsum("rghd,rpgd->rghp", query_heads, cached_keys, preferred_element_type=jnp.float32)
        * scale
    )
    fresh_scores = (
        jnp.einsum("rghd,rgd->rgh", query_heads, fresh_keys, preferred_element_type=jnp.float32)
        * scale
    )
    valid_mask = (jnp.arange(CTX, dtype=jnp.int32)[None, :] < cache_length[:, None])[
        :, None, None, :
    ]
    masked = jnp.where(valid_mask, scores, -jnp.inf)
    top_score = jnp.maximum(jnp.max(masked, axis=3), fresh_scores)
    raw_weights = jnp.where(valid_mask, jnp.exp(scores - top_score[..., None]), 0.0)
    fresh_raw = jnp.exp(fresh_scores - top_score)
    norm_total = jnp.sum(raw_weights, axis=3) + fresh_raw
    weights = (raw_weights / norm_total[..., None]).astype(jnp.bfloat16)
    fresh_weights = (fresh_raw / norm_total).astype(jnp.bfloat16)
    result_sum = jnp.einsum(
        "rghp,rpgd->rghd", weights, cached_values, preferred_element_type=jnp.float32
    )
    result_sum = (
        result_sum
        + fresh_weights.astype(jnp.float32)[..., None]
        * fresh_values.astype(jnp.float32)[:, :, None, :]
    )
    return result_sum.astype(jnp.bfloat16).reshape(row_count, queries.shape[1])


def body(
    features,
    value_matrix,
    adapter_down,
    adapter_up,
    queries,
    new_key_rows,
    stored_key_cache,
    stored_value_cache,
    cache_length,
    resident_adapter_index,
    panel_owner_slot,
    outgoing_rows,
    outgoing_counts,
):
    replica_count = lax.axis_size("replica")
    row_half = resident_adapter_index.shape[0]
    local_adapters, adapter_rank_size, half_width = adapter_down.shape
    column_half = adapter_up.shape[2]
    adapter_range = jnp.arange(local_adapters, dtype=jnp.int32)
    base_portion = jnp.dot(features, value_matrix, preferred_element_type=jnp.float32)
    down_flattened = adapter_down.reshape(local_adapters * adapter_rank_size, half_width)
    down_panels = adapter_down.reshape(local_adapters, adapter_rank_size * half_width)
    up_flattened = adapter_up.reshape(local_adapters, adapter_rank_size * column_half)
    resident_rows = features[:row_half]
    incoming_rows = features[row_half:]
    partial_products = lax.dot_general(
        resident_rows, down_flattened, (((1,), (1,)), ((), ())), preferred_element_type=jnp.float32
    )
    partial_products = partial_products.reshape(row_half, local_adapters, adapter_rank_size)
    chooser = (resident_adapter_index[:, None] == adapter_range[None, :]).astype(jnp.float32)
    shrink_resident = jnp.sum(partial_products * chooser[:, :, None], axis=1)
    resident_up_weight = jnp.dot(
        chooser.astype(jnp.bfloat16), up_flattened, preferred_element_type=jnp.float32
    )
    resident_up_weight = resident_up_weight.reshape(row_half, adapter_rank_size, column_half)
    outgoing_table = outgoing_rows[0]
    counts = outgoing_counts[0]
    live_mask = jnp.arange(PANEL_SLOTS, dtype=jnp.int32)[None, :] < counts[:, None]
    selector = (outgoing_table[:, :, None] == adapter_range[None, None, :]) & live_mask[:, :, None]
    selector = selector.astype(jnp.bfloat16).reshape(replica_count * PANEL_SLOTS, local_adapters)
    down_send = jnp.dot(selector, down_panels, preferred_element_type=jnp.bfloat16)
    down_send = down_send.reshape(replica_count, PANEL_SLOTS, adapter_rank_size * half_width)
    up_send = jnp.dot(selector, up_flattened, preferred_element_type=jnp.bfloat16)
    up_send = up_send.reshape(replica_count, PANEL_SLOTS, adapter_rank_size * column_half)
    received_down, received_up = (
        lax.all_to_all(down_send, "replica", split_axis=0, concat_axis=0, tiled=True),
        lax.all_to_all(up_send, "replica", split_axis=0, concat_axis=0, tiled=True),
    )
    panel_count = replica_count * PANEL_SLOTS
    all_products = lax.dot_general(
        incoming_rows,
        received_down.reshape(panel_count * adapter_rank_size, half_width),
        (((1,), (1,)), ((), ())),
        preferred_element_type=jnp.float32,
    )
    all_products = all_products.reshape(row_half, panel_count, adapter_rank_size)
    picker = panel_owner_slot[:, None] == jnp.arange(panel_count, dtype=jnp.int32)[None, :]
    shrink_new = jnp.sum(all_products * picker.astype(jnp.float32)[:, :, None], axis=1)
    new_up_weight = jnp.dot(
        picker.astype(jnp.bfloat16),
        received_up.reshape(panel_count, adapter_rank_size * column_half),
        preferred_element_type=jnp.float32,
    )
    new_up_weight = new_up_weight.reshape(row_half, adapter_rank_size, column_half)
    shrink_local = jnp.concatenate([shrink_resident, shrink_new], axis=0)
    base_local = lax.psum_scatter(base_portion, "tensor", scatter_dimension=1, tiled=True)
    shrunk_input = lax.psum(shrink_local, "tensor")
    output_resident = jnp.einsum(
        "sj,sjo->so", shrunk_input[:row_half], resident_up_weight, precision=lax.Precision.HIGHEST
    )
    output_new = jnp.einsum(
        "sj,sjo->so", shrunk_input[row_half:], new_up_weight, precision=lax.Precision.HIGHEST
    )
    adapter_output = jnp.concatenate([output_resident, output_new], axis=0)
    new_value_rows = (base_local + ADAPTER_SCALE * adapter_output).astype(jnp.bfloat16)
    attended = attend(
        queries, new_key_rows, stored_key_cache, stored_value_cache, new_value_rows, cache_length
    )
    return (new_value_rows, attended)


def solution(mesh):
    in_specs = (
        P(("groups", "replica"), "tensor"),
        P("tensor", None),
        P("replica", None, "tensor"),
        P("replica", None, "tensor"),
        P(("groups", "replica"), "tensor"),
        P(("groups", "replica"), "tensor"),
        P(("groups", "replica"), None, "tensor"),
        P(("groups", "replica"), None, "tensor"),
        P(("groups", "replica")),
        P(("groups", "replica")),
        P(("groups", "replica")),
        P(("groups", "replica"), None, None),
        P(("groups", "replica"), None),
    )
    out_specs = (P(("groups", "replica"), "tensor"), P(("groups", "replica"), "tensor"))
    return jax.shard_map(body, mesh=mesh, in_specs=in_specs, out_specs=out_specs, check_vma=False)
```

profile of v0, /device:TPU:0, one launch (start us, length us, event | category | flops | bytes accessed | tf_op | source)
XLA Modules:
  0.0 116.6 jit_solution(5681853030237863485)
XLA Ops:
  7.2 0.0 copy-start
  7.2 0.8 iota_compare_fusion.4
  8.0 0.9 reshape.212
  8.9 0.9 fusion.42
  9.8 0.8 copy.57
  10.6 7.3 %all-to-all-start.1 = ((bf16[8,2,4096]{2,1,0:T(2,128)(2,1)}), bf16[8,2,4096]{2,1,0:T(2,128)(2,1)}, u32[]{:S(2)}, u32[]{:S(2)}) async-start(bf16[8,2,4096]{2,1,0:T(2,128)(2,1)} %copy.57), calls=%async_computation.2 | async-start | bytes 262144 | tf_op jit(solution)/shard_map/all_to_all | solution.py:102
  17.9 2.2 %reshape.208 = bf16[4,65536,1]{1,0,2:T(4,128)(2,1)} reshape(bf16[4,16,4096]{2,1,0:T(8,128)(2,1)} %param.15) | data formatting | bytes 1048576 | tf_op jit(solution)/shard_map/reshape | solution.py:77
  20.1 1.8 %fusion.44 = bf16[8,2,65536]{2,0,1:T(8,128)(2,1)S(1)} fusion(bf16[4,65536,1]{1,0,2:T(4,128)(2,1)} %reshape.208, s32[8,2]{0,1:T(2,128)} %bitcast.103, pred[8,2]{0,1:T(4,128)(4,1)S(1)} %iota_compare_fusion.4), kind=kOutput, calls=%fused_computation.55 | convolution fusion | flops 8388736 | bytes 2621520 | tf_op jit(solution)/shard_map/dot_general | solution.py:96
  21.9 0.0 copy-start.1
  22.0 3.5 %copy.53 = bf16[8,2,65536]{2,1,0:T(2,128)(2,1)} copy(bf16[8,2,65536]{2,0,1:T(8,128)(2,1)S(1)} %fusion.44) | data formatting | bytes 4194304 | tf_op jit(solution)/shard_map/dot_general | solution.py:96
  25.4 0.0 all-to-all-done.1
  25.4 6.0 %all-to-all-start = ((bf16[8,2,65536]{2,1,0:T(2,128)(2,1)}), bf16[8,2,65536]{2,1,0:T(2,128)(2,1)}, u32[]{:S(2)}, u32[]{:S(2)}) async-start(bf16[8,2,65536]{2,1,0:T(2,128)(2,1)} %copy.53), calls=%async_computation.1 | async-start | bytes 4194304 | tf_op jit(solution)/shard_map/all_to_all | solution.py:101
  31.4 0.0 copy-start.5
  31.4 0.0 copy-start.6
  31.4 0.0 reduce-scatter.2.cloned.1.call-start
  31.5 0.0 copy-done.1
  31.5 3.7 %fusion.58 = f32[48,512]{1,0:T(8,128)} fusion(bf16[48,4096]{1,0:T(8,128)(2,1)S(1)} %copy-done.1, bf16[4096,512]{1,0:T(8,128)(2,1)} %param.14), kind=kOutput, calls=%fused_computation.69 | convolution fusion | flops 201326592 | bytes 4685824 | tf_op jit(solution)/shard_map/dot_general | solution.py:75
  35.2 0.0 reduce-scatter.2.cloned.1.call-update
  35.2 0.0 copy-done.5
  35.2 0.7 copy.54
  35.9 1.0 copy.78
  36.8 0.0 copy-done.6
  36.8 0.0 copy-start.2
  36.8 0.1 iota_compare_fusion
  36.9 0.0 copy-start.3
  36.9 0.6 copy-done.2
  37.5 0.0 copy-done
  37.5 2.5 %select_reduce_fusion = (f32[48,2,8]{2,1,0:T(2,128)}, f32[48,2,8,128]{3,2,1,0:T(8,128)S(1)}) fusion(pred[48,128]{1,0:T(8,128)(4,1)S(1)} %iota_compare_fusion, bf16[48,2,8,128]{3,2,1,0:T(8,128)(2,1)S(1)} %bitcast.95, bf16[48,128,256]{2,1,0:T(8,128)(2,1)S(1)} %copy-done), kind=kOutput, calls=%fused_computation.18 | convolution fusion | flops 25459968 | bytes 3744768 | tf_op jit(solution)/shard_map/rghd,rpgd->rghp/dot_general | solution.py:27
  40.0 0.0 copy-done.3
  40.0 0.9 copy.60
  40.9 1.4 %reshape.221 = bf16[48,2,128,1]{2,3,1,0:T(2,128)(2,1)} reshape(bf16[48,256]{1,0:T(8,128)(2,1)} %param.18) | data formatting | bytes 49152 | tf_op jit(solution)/shard_map/reshape | solution.py:23
  42.3 1.8 %fusion.59 = f32[48,2,1,8]{3,2,1,0:T(1,128)} fusion(bf16[48,2,8,128]{3,2,1,0:T(8,128)(2,1)} %bitcast.96, bf16[48,2,128,1]{2,3,1,0:T(2,128)(2,1)} %reshape.221), kind=kOutput, calls=%fused_computation.70 | convolution fusion | flops 196608 | bytes 224256 | tf_op jit(solution)/shard_map/rghd,rgd->rgh/dot_general | solution.py:31
  44.0 0.9 copy.73
  44.9 0.6 fusion.36
  45.5 1.4 %copy.61 = f32[48,2,8]{2,1,0:T(2,128)} copy(f32[48,2,8]{0,2,1:T(8,128)} %fusion.36) | data formatting | bytes 6144 | tf_op jit(solution)/shard_map/max | solution.py:38
  46.9 1.7 %fusion.20 = f32[48,2,8]{2,1,0:T(2,128)} fusion(f32[48,2,8,128]{3,2,1,0:T(8,128)S(1)} %get-tuple-element.7, f32[48,2,8]{2,1,0:T(2,128)} %copy.61, pred[48,128]{1,0:T(8,128)(4,1)} %copy-done.3), kind=kLoop, calls=%fused_computation.19 | loop fusion | flops 294144 | bytes 405504 | tf_op jit(solution)/shard_map/reduce_sum | solution.py:41
  48.7 1.5 %copy.62 = f32[48,2,8]{0,2,1:T(8,128)} copy(f32[48,2,8]{2,1,0:T(2,128)} %fusion.20) | data formatting | bytes 6144 | tf_op jit(solution)/shard_map/reduce_sum | solution.py:41
  50.1 1.3 %fusion.41 = (f32[48,2,8]{0,2,1:T(8,128)}, f32[48,2,8]{0,2,1:T(8,128)}) fusion(f32[48,2,8]{0,2,1:T(8,128)} %copy.62, f32[48,2,1,8]{0,3,1,2:T(8,128)S(1)} %copy.73, f32[48,2,8]{0,2,1:T(8,128)S(1)} %copy.60), kind=kLoop, calls=%fused_computation.53 | loop fusion | flops 5376 | bytes 15360 | tf_op jit(solution)/shard_map/add | solution.py:41
  51.5 1.4 %copy.65 = f32[48,2,8]{2,1,0:T(2,128)} copy(f32[48,2,8]{0,2,1:T(8,128)} %get-tuple-element.3) | data formatting | bytes 6144 | tf_op jit(solution)/shard_map/convert_element_type | solution.py:49
  52.9 1.4 %copy.63 = f32[48,2,8]{2,1,0:T(2,128)} copy(f32[48,2,8]{0,2,1:T(8,128)} %get-tuple-element.2) | data formatting | bytes 6144 | tf_op jit(solution)/shard_map/add | solution.py:41
  54.3 0.7 fusion.48
  54.9 2.0 %fusion.15 = f32[24,16]{0,1:T(8,128)} fusion(bf16[4,16,4096]{2,1,0:T(8,128)(2,1)} %param.15, bf16[48,4096]{1,0:T(8,128)(2,1)} %param.13, f32[24,4]{0,1:T(4,128)S(1)} %fusion.48), kind=kOutput, calls=%fused_computation.11 | convolution fusion | flops 12585600 | bytes 722816 | tf_op jit(solution)/shard_map/dot_general | solution.py:81
  56.9 1.8 %fusion.51 = f32[24,16,256]{2,0,1:T(8,128)} fusion(s32[24]{0:T(128)} %param.22, bf16[1,4,16,256]{3,2,1,0:T(8,128)(2,1)} %bitcast.101), kind=kOutput, calls=%fused_computation.62 | convolution fusion | flops 786720 | bytes 426080 | tf_op jit(solution)/shard_map/dot_general | solution.py:87
  58.7 1.6 %reshape.200 = bf16[16,4096]{1,0:T(8,128)(2,1)} reshape(bf16[8,2,4096]{2,1,0:T(2,128)(2,1)} %all-to-all-done.1) | data formatting | bytes 262144 | tf_op jit(solution)/shard_map/reshape | solution.py:116
  60.3 1.9 %fusion.28 = f32[24,16,256]{2,0,1:T(8,128)} fusion(bf16[2,16,8,256]{3,2,1,0:T(8,128)(2,1)} %bitcast.97, s32[24]{0:T(128)} %param.23), kind=kOutput, calls=%fused_computation.29 | convolution fusion | flops 3146112 | bytes 524384 | tf_op jit(solution)/shard_map/dot_general | solution.py:114
  62.3 16.9 %all-to-all-done = bf16[8,2,65536]{2,1,0:T(2,128)(2,1)} async-done(((bf16[8,2,65536]{2,1,0:T(2,128)(2,1)}), bf16[8,2,65536]{2,1,0:T(2,128)(2,1)}, u32[]{:S(2)}, u32[]{:S(2)}) %all-to-all-start) | async-done | bytes 2097184 | tf_op jit(solution)/shard_map/all_to_all | solution.py:101
  79.2 6.4 %reshape.197 = bf16[256,4096]{1,0:T(8,128)(2,1)} reshape(bf16[8,2,65536]{2,1,0:T(2,128)(2,1)} %all-to-all-done) | data formatting | bytes 4194304 | tf_op jit(solution)/shard_map/reshape | solution.py:107
  85.6 2.9 %convolution_bitcast_fusion = f32[24,256]{1,0:T(8,128)} fusion(bf16[256,4096]{1,0:T(8,128)(2,1)} %reshape.197, bf16[48,4096]{1,0:T(8,128)(2,1)} %param.13), kind=kOutput, calls=%fused_computation.10 | convolution fusion | flops 50331648 | bytes 2318336 | tf_op jit(solution)/shard_map/dot_general | solution.py:105
  88.4 1.5 %reshape.198 = f32[24,16,16]{2,1,0:T(8,128)} reshape(f32[24,256]{1,0:T(8,128)} %convolution_bitcast_fusion) | data formatting | bytes 49152 | tf_op jit(solution)/shard_map/reshape | solution.py:111
  90.0 1.7 %multiply_reduce_fusion = f32[24,16]{1,0:T(8,128)} fusion(f32[24,16,16]{2,1,0:T(8,128)} %reshape.198, f32[24,16]{1,0:T(8,128)} %copy.54), kind=kLoop, calls=%fused_computation.25 | loop fusion | flops 11904 | bytes 27648 | tf_op jit(solution)/shard_map/reduce_sum | solution.py:113
  91.6 0.8 copy.55
  92.4 1.4 %pad_maximum_fusion = f32[48,16]{0,1:T(8,128)} fusion(f32[24,16]{0,1:T(8,128)S(1)} %copy.55, f32[24,16]{0,1:T(8,128)} %fusion.15), kind=kLoop, calls=%fused_computation.40 | loop fusion | flops 768 | bytes 6144 | tf_op jit(solution)/shard_map/concatenate | solution.py:120
  93.8 2.6 %psum.7 = f32[48,16]{0,1:T(8,128)S(1)} all-reduce(f32[48,16]{0,1:T(8,128)} %pad_maximum_fusion), channel_id=1, replica_groups=mesh['groups'=2,'replica'=8,'tensor'=2] {'tensor'}, use_global_device_ids=true, to_apply=%region_3.0 | all-reduce | flops 768 | bytes 6144 | tf_op jit(solution)/shard_map/psum | solution.py:122
  96.4 0.7 slice_bitcast_fusion.1
  97.0 1.4 %copy.69 = f32[24,16,1]{1,2,0:T(1,128)} copy(f32[24,16,1]{0,1,2:T(8,128)} %get-tuple-element.5) | data formatting | bytes 3072 | tf_op jit(solution)/shard_map/slice | solution.py:127
  98.4 1.4 %copy.66 = f32[24,16,1]{1,2,0:T(1,128)} copy(f32[24,16,1]{0,1,2:T(8,128)} %get-tuple-element.4) | data formatting | bytes 3072 | tf_op jit(solution)/shard_map/slice | solution.py:124
  99.8 1.4 %fusion.16 = f32[24,1,256]{2,1,0:T(1,128)S(1)} fusion(f32[24,16,1]{1,2,0:T(1,128)} %copy.69, f32[24,16,256]{2,0,1:T(8,128)} %fusion.28), kind=kOutput, calls=%fused_computation.12 | convolution fusion | flops 1179648 | bytes 419328 | tf_op jit(solution)/shard_map/sj,sjo->so/dot_general | solution.py:126
  101.2 1.4 %fusion.18 = f32[24,1,256]{2,1,0:T(1,128)S(1)} fusion(f32[24,16,1]{1,2,0:T(1,128)} %copy.66, f32[24,16,256]{2,0,1:T(8,128)} %fusion.51), kind=kOutput, calls=%fused_computation.14 | convolution fusion | flops 1179648 | bytes 419328 | tf_op jit(solution)/shard_map/sj,sjo->so/dot_general | solution.py:123
  102.7 0.6 copy_bitcast_fusion.1
  103.3 1.4 %fusion.32 = bf16[48,256]{1,0:T(8,128)(2,1)} fusion(f32[48,256]{1,0:T(8,128)} %reduce-scatter.2.cloned.1.call-done, f32[24,256]{1,0:T(8,128)} %get-tuple-element.8, f32[24,256]{1,0:T(8,128)} %get-tuple-element.9), kind=kLoop, calls=%fused_computation.34 | loop fusion | flops 49152 | bytes 122880 | tf_op jit(solution)/shard_map/convert_element_type | solution.py:130
  104.7 1.4 %reshape.206 = f32[48,2,128]{2,1,0:T(2,128)} reshape(bf16[48,256]{1,0:T(8,128)(2,1)} %fusion.32) | data formatting | bytes 73728 | tf_op jit(solution)/shard_map/convert_element_type | solution.py:50
  106.1 0.0 copy-done.4
  106.1 3.0 %fusion.12 = bf16[48,2,8,128]{3,2,1,0:T(8,128)(2,1)S(1)} fusion(f32[48,2,8,128]{3,2,1,0:T(8,128)S(1)} %get-tuple-element.7, f32[48,2,128]{2,1,0:T(2,128)} %reshape.206, f32[48,2,8]{2,1,0:T(2,128)} %copy.65, f32[48,2,8]{2,1,0:T(2,128)} %copy.63, f32[48,2,8]{2,1,0:T(2,128)} %copy.61, pred[48,128]{1,0:T(8,128)(4,1)S(1)} %copy-done.4, ...), kind=kOutput, calls=%fused_computation.8 | convolution fusion | flops 25853952 | bytes 3800064 | tf_op jit(solution)/shard_map/rghp,rpgd->rghd/dot_general | solution.py:44
  109.1 0.7 copy.111
  (3 shorter events, 0.0 us)
Async XLA Ops:
  7.2 30.4 %copy-start = (bf16[48,128,256]{2,1,0:T(8,128)(2,1)S(1)}, bf16[48,128,256]{2,1,0:T(8,128)(2,1)}, u32[]{:S(2)}) copy-start(bf16[48,128,256]{2,1,0:T(8,128)(2,1)} %param.19) | copy-start | bytes 9437188
  10.6 14.8 %all-to-all-start.1 = ((bf16[8,2,4096]{2,1,0:T(2,128)(2,1)}), bf16[8,2,4096]{2,1,0:T(2,128)(2,1)}, u32[]{:S(2)}, u32[]{:S(2)}) async-start(bf16[8,2,4096]{2,1,0:T(2,128)(2,1)} %copy.57), calls=%async_computation.2 | async-start | bytes 262144 | tf_op jit(solution)/shard_map/all_to_all | solution.py:102
  21.9 9.5 %copy-start.1 = (bf16[48,4096]{1,0:T(8,128)(2,1)S(1)}, bf16[48,4096]{1,0:T(8,128)(2,1)}, u32[]{:S(2)}) copy-start(bf16[48,4096]{1,0:T(8,128)(2,1)} %param.13) | copy-start | bytes 1179652
  25.4 53.8 %all-to-all-start = ((bf16[8,2,65536]{2,1,0:T(2,128)(2,1)}), bf16[8,2,65536]{2,1,0:T(2,128)(2,1)}, u32[]{:S(2)}, u32[]{:S(2)}) async-start(bf16[8,2,65536]{2,1,0:T(2,128)(2,1)} %copy.53), calls=%async_computation.1 | async-start | bytes 4194304 | tf_op jit(solution)/shard_map/all_to_all | solution.py:101
  31.4 3.8 %copy-start.5 = (s32[24]{0:T(128)S(1)}, s32[24]{0:T(128)}, u32[]{:S(2)}) copy-start(s32[24]{0:T(128)} %param.23) | copy-start | bytes 292
  31.4 5.4 %copy-start.6 = (s32[48]{0:T(128)S(1)}, s32[48]{0:T(128)}, u32[]{:S(2)}) copy-start(s32[48]{0:T(128)} %param.21) | copy-start | bytes 580
  31.4 71.9 %reduce-scatter.2.cloned.1.call-start = ((), (), s32[]{:S(2)}) async-start(), calls=%async_computation.3 | async-start | bytes 147456 | tf_op jit(solution)/shard_map/reduce_scatter | solution.py:121
  36.8 0.7 copy-start.2
  36.9 3.1 %copy-start.3 = (pred[48,128]{1,0:T(8,128)(4,1)}, pred[48,128]{1,0:T(8,128)(4,1)S(1)}, u32[]{:S(2)}) copy-start(pred[48,128]{1,0:T(8,128)(4,1)S(1)} %iota_compare_fusion) | copy-start | bytes 18436
  62.3 43.8 %copy-start.4 = (pred[48,128]{1,0:T(8,128)(4,1)S(1)}, pred[48,128]{1,0:T(8,128)(4,1)}, u32[]{:S(2)}) copy-start(pred[48,128]{1,0:T(8,128)(4,1)} %copy-done.3) | copy-start | bytes 18436
Sparse Core Ops, SparseCore 0:
  35.3 8.8 reduce-scatter.1
where the time goes:
time: 118 us; the launch traced here: 117 us
  local copies, waits for them, and re-layouts  34.8 us (29%)
  matrix products  25.1 us (21%)
  waiting for transfers between devices  17 us (14%)
  between operations  14.2 us (12%)
  starting transfers between devices  13.3 us (11%)
  other arithmetic  9.67 us (8%)
  blocking collectives  2.59 us (2%)
    all_to_all x1, waiting for transfers between devices, body(): lax.all_to_all(down_send, 'replica', split_axis=0, concat_axis=0, tiled=T...  16.9 us
    all_to_all x1, starting transfers between devices, body(): lax.all_to_all(up_send, 'replica', split_axis=0, concat_axis=0, tiled=True)  7.28 us
    reshape x1, local copies, waits for them, and re-layouts, body(): received_down.reshape(panel_count * adapter_rank_size, half_width)  6.36 us
    all_to_all x1, starting transfers between devices, body(): lax.all_to_all(down_send, 'replica', split_axis=0, concat_axis=0, tiled=T...  6 us
    dot_general x1, matrix products, body(): jnp.dot(features, value_matrix, preferred_element_type=jnp.float32)  3.66 us
    dot_general x1, local copies, waits for them, and re-layouts, body(): jnp.dot(selector, down_panels, preferred_element_type=jnp.bfloat16)  3.46 us
    dot_general x1, matrix products, attend(): jnp.einsum('rghp,rpgd->rghd', weights, cached_values, preferred_element_t...  2.96 us
    dot_general x1, matrix products, body(): lax.dot_general(incoming_rows, received_down.reshape(panel_count * adapte...  2.87 us
  transfers between devices with their start and end apart: 3, of which 1 were waited for; matrix products, arithmetic and copies ran while one was open for 51% of the time, Pallas kernels for 0%

commit v1 on v0

v1 whole, which is shorter than its diff:
```python
import functools
import math

import jax
import jax.numpy as jnp
from jax import lax
from jax.experimental import pallas as pl
from jax.experimental.pallas import tpu as pltpu
from jax.sharding import PartitionSpec as P

HD = 128
PANEL_SLOTS = 2
ADAPTER_SCALE = 2.0
MESH = pl.DeviceIdType.MESH
F32, BF16, I32 = jnp.float32, jnp.bfloat16, jnp.int32
NT = (((1,), (1,)), ((), ()))
RANKS = 4
CHUNKS = 4


def iota(shape, axis):
    return lax.broadcasted_iota(I32, shape, axis)


def dot(a, b, dims=(((1,), (0,)), ((), ()))):
    return lax.dot_general(a, b, dims, preferred_element_type=F32)


def split(x):
    high = x.astype(BF16)
    return high, (x - high.astype(F32)).astype(BF16)


def spread(ref, count, shape, axis, first):
    index = iota(shape, axis)
    out = jnp.full(shape, -1, I32)
    for i in range(count):
        out = jnp.where(index == first + i, ref[i], out)
    return out


def kernel(
    replicas, per_pair, pieces,
    feat_hbm, vm_hbm, down_hbm, up_hbm, q_hbm, nk_hbm, k_hbm, v_hbm,
    len_ref, res_ref, slot_ref, rows_ref, count_ref,
    nv_ref, att_ref,
    feat, vm, down, up, q, nk, kc, vc,
    x32, tx, rx, half_tx, half_rx, shr_tx, shr_rx, ret_tx, ret_rx,
    q3, nk3, sc, wt, fresh, acc,
    in_sem, vm_sem, k_sem, v_sem, tx_sem, rx_sem, ret_tx_sem, ret_rx_sem, peer_sem,
):
    me = lax.axis_index("replica")
    core = lax.axis_index("tensor")
    rows, width = feat.shape
    half = res_ref.shape[0]
    adapters, rank, _ = down.shape
    flat = adapters * rank
    cols = up.shape[2]
    kv = nk.shape[1] // HD
    heads = q.shape[1] // HD
    group = heads // kv
    ctx = kc.shape[1]
    piece = width // pieces
    sent = replicas * per_pair
    block = PANEL_SLOTS * RANKS
    step = rows // CHUNKS
    depth = width // CHUNKS

    def load(src, dst, sem):
        copy = pltpu.make_async_copy(src, dst, sem)
        copy.start()
        return copy

    feat_in = load(feat_hbm, feat, in_sem.at[0])
    down_in = load(down_hbm, down, in_sem.at[1])
    vm_in = [
        load(vm_hbm.at[pl.ds(c * depth, depth)], vm.at[pl.ds(c * depth, depth)], vm_sem.at[c])
        for c in range(CHUNKS)
    ]
    q_in = load(q_hbm, q, in_sem.at[2])
    nk_in = load(nk_hbm, nk, in_sem.at[3])
    k_in = [
        load(k_hbm.at[pl.ds(c * step, step)], kc.at[pl.ds(c * step, step)], k_sem.at[c])
        for c in range(CHUNKS)
    ]
    up_in = load(up_hbm, up, in_sem.at[4])
    v_in = [
        load(v_hbm.at[pl.ds(c * step, step)], vc.at[pl.ds(c * step, step)], v_sem.at[c])
        for c in range(CHUNKS)
    ]

    barrier = pltpu.get_barrier_semaphore()
    for d in range(1, replicas):
        pl.semaphore_signal(
            barrier, inc=1, device_id={"replica": lax.rem(me + d, replicas)}, device_id_type=MESH
        )
    pl.semaphore_signal(barrier, inc=1, device_id={"tensor": 1 - core}, device_id_type=MESH)

    square = (rows, rows)
    sub, lane = iota(square, 0), iota(square, 1)
    slot_l = spread(slot_ref, half, square, 1, half)
    slot_s = spread(slot_ref, half, square, 0, half)
    own_l, own_s = slot_l >> 1, slot_s >> 1
    same = own_l == own_s
    number_l = jnp.sum(jnp.where(same & (sub < lane), 1.0, 0.0), axis=0, keepdims=True).astype(I32)
    number_s = jnp.sum(jnp.where(same & (lane < sub), 1.0, 0.0), axis=1, keepdims=True).astype(I32)
    goes = jnp.where(lane[:1] >= half, own_l[:1] * per_pair + number_l, -1)
    chooser = jnp.where(iota((sent, rows), 0) == goes, 1.0, 0.0).astype(BF16)
    comes = own_s[:, :1] * block + (slot_s[:, :1] & 1) * RANKS + number_s
    comes = jnp.where(sub[:, :1] >= half, comes, -1)
    picker = jnp.where(iota((rows, replicas * block), 1) == comes, 1.0, 0.0).astype(BF16)

    feat_in.wait()
    chosen = dot(chooser, feat[...])
    lanes = piece // HD
    for p in range(pieces):
        for b in range(lanes):
            at = p * piece + b * HD
            x32[b, pl.ds(p, sent, stride=pieces), :] = chosen[:, at : at + HD]
    for b in range(lanes):
        tx[:, :, b * HD : (b + 1) * HD] = x32[b].astype(BF16).reshape(replicas, -1, HD)

    pl.semaphore_wait(barrier, replicas)
    out_copies = []
    for d in range(1, replicas):
        there = lax.rem(me + d, replicas)
        copy = pltpu.make_async_remote_copy(
            src_ref=tx.at[there], dst_ref=rx.at[me],
            send_sem=tx_sem.at[d], recv_sem=rx_sem.at[d],
            device_id={"replica": there}, device_id_type=MESH,
        )
        copy.start()
        out_copies.append(copy)
    rx[me] = tx[me]

    down_in.wait()
    shrunk = dot(feat[...], down[...].reshape(flat, width), NT)
    res_s = spread(res_ref, half, (rows, flat), 0, 0)
    shrunk = jnp.where((iota((rows, flat), 1) // rank) == res_s, shrunk, 0.0)[:half]
    base = jnp.zeros((rows, 2 * cols), F32)
    for c in range(CHUNKS):
        vm_in[c].wait()
        base += dot(feat[:, c * depth : (c + 1) * depth], vm[c * depth : (c + 1) * depth, :])
    padded = jnp.concatenate([shrunk, jnp.zeros((half, cols - flat), F32)], axis=1)
    for t in range(2):
        half_tx[t, :rows] = base[:, t * cols : (t + 1) * cols]
        half_tx[t, rows:] = padded
    half_copy = pltpu.make_async_remote_copy(
        src_ref=half_tx.at[1 - core], dst_ref=half_rx,
        send_sem=peer_sem.at[0], recv_sem=peer_sem.at[1],
        device_id={"tensor": 1 - core}, device_id_type=MESH,
    )
    half_copy.start()

    q_in.wait()
    nk_in.wait()
    for h in range(heads):
        g = h // group
        q3[pl.ds(h, rows, stride=heads), :] = q[:, h * HD : (h + 1) * HD].astype(F32)
        nk3[pl.ds(h, rows, stride=heads), :] = nk[:, g * HD : (g + 1) * HD].astype(F32)
    scale = 1.0 / math.sqrt(HD)
    head_of = iota((heads, HD), 0) // group
    place = iota((heads, ctx), 1)
    unroll = 6

    def score(base_row):
        for u in range(unroll):
            r = base_row + u
            rows_r = q3[pl.ds(pl.multiple_of(r * heads, heads), heads), :]
            wide = jnp.concatenate(
                [jnp.where(head_of == g, rows_r, 0.0) for g in range(kv)], axis=1
            ).astype(BF16)
            s = dot(wide, kc[r], NT) * scale
            sc[r] = jnp.where(place < len_ref[r], s, -jnp.inf)

    for c in range(CHUNKS):
        k_in[c].wait()
        lax.fori_loop(
            0, step // unroll, lambda i, _, c=c: score(c * step + i * unroll), None
        )

    for copy in out_copies:
        copy.wait_recv()
    for b in range(lanes):
        x32[b] = rx[:, :, b * HD : (b + 1) * HD].reshape(sent * pieces, HD).astype(F32)
    foreign = jnp.zeros((sent, flat), F32)
    for p in range(pieces):
        x_p = [x32[b, pl.ds(p, sent, stride=pieces), :] for b in range(lanes)]
        x_p = jnp.concatenate(x_p, axis=1).astype(BF16)
        foreign += dot(x_p, down[:, :, p * piece : (p + 1) * piece].reshape(flat, piece), NT)
    shr_tx[...] = jnp.concatenate([foreign, jnp.zeros((sent, HD - flat), F32)], axis=1)
    shr_copy = pltpu.make_async_remote_copy(
        src_ref=shr_tx, dst_ref=shr_rx,
        send_sem=peer_sem.at[2], recv_sem=peer_sem.at[3],
        device_id={"tensor": 1 - core}, device_id_type=MESH,
    )
    shr_copy.start()

    def soften(c):
        r = pl.ds(c * step, step)
        flat_r = pl.ds(c * step * heads, step * heads)
        s = sc[r].reshape(step * heads, ctx)
        fs = jnp.sum(q3[flat_r, :] * nk3[flat_r, :], axis=1, keepdims=True) * scale
        top = jnp.maximum(jnp.max(s, axis=1, keepdims=True), fs)
        w = jnp.exp(s - top)
        fw = jnp.exp(fs - top)
        inverse = 1.0 / (jnp.sum(w, axis=1, keepdims=True) + fw)
        wt[r] = (w * inverse).astype(BF16).reshape(step, heads, ctx)
        fw = (fw * inverse).astype(BF16).astype(F32)
        fresh[flat_r, :] = jnp.broadcast_to(fw, (step * heads, HD))

    for c in range(CHUNKS):
        soften(c)

    up_in.wait()
    shape = (replicas * block, flat)
    sub, lane = iota(shape, 0), iota(shape, 1)
    adapter = jnp.full(shape, -1, I32)
    for i in range(replicas):
        for s in range(PANEL_SLOTS):
            at = (sub // RANKS) == i * PANEL_SLOTS + s
            value = jnp.where(s < count_ref[0, i], rows_ref[0, i, s], -1)
            adapter = jnp.where(at, value, adapter)
    shape = (replicas * block, sent)
    sub_e, lane_e = iota(shape, 0), iota(shape, 1)
    place_e = sub_e & (RANKS - 1)
    expand = ((sub_e // block) * per_pair + place_e == lane_e) & (place_e < per_pair)
    expand = jnp.where(expand, 1.0, 0.0).astype(BF16)
    up_flat = up[...].reshape(flat, cols)
    shr_copy.wait_recv()
    high, low = split(shr_tx[:, :flat] + shr_rx[:, :flat])
    keep = (lane // rank) == adapter
    high = jnp.where(keep, dot(expand, high), 0.0).astype(BF16)
    low = jnp.where(keep, dot(expand, low), 0.0).astype(BF16)
    ret_tx[...] = (dot(high, up_flat) + dot(low, up_flat)).reshape(ret_tx.shape)
    ret_copies = []
    for d in range(1, replicas):
        there = lax.rem(me + d, replicas)
        copy = pltpu.make_async_remote_copy(
            src_ref=ret_tx.at[there], dst_ref=ret_rx.at[me],
            send_sem=ret_tx_sem.at[d], recv_sem=ret_rx_sem.at[d],
            device_id={"replica": there}, device_id_type=MESH,
        )
        copy.start()
        ret_copies.append(copy)
    ret_rx[me] = ret_tx[me]

    def gather(base_row):
        for u in range(unroll):
            r = base_row + u
            mixed = dot(wt[r], vc[r])
            out = mixed[:, :HD]
            for g in range(1, kv):
                out = jnp.where(head_of == g, mixed[:, g * HD : (g + 1) * HD], out)
            acc[pl.ds(pl.multiple_of(r * heads, heads), heads), :] = out

    for c in range(CHUNKS):
        v_in[c].wait()
        lax.fori_loop(
            0, step // unroll, lambda i, _, c=c: gather(c * step + i * unroll), None
        )

    half_copy.wait_recv()
    both = half_tx[core] + half_rx[...]
    high, low = split(both[rows:, :flat])
    resident = dot(high, up_flat) + dot(low, up_flat)
    resident = jnp.concatenate([resident, jnp.zeros((rows - half, cols), F32)], axis=0)
    for copy in ret_copies:
        copy.wait_recv()
    high, low = split(ret_rx[...].reshape(replicas * block, cols))
    adapted = resident + (dot(picker, high) + dot(picker, low))
    values = (both[:rows] + ADAPTER_SCALE * adapted).astype(BF16)
    nv_ref[...] = values
    values = values.astype(F32)
    for h in range(heads):
        g = h // group
        at = pl.ds(h, rows, stride=heads)
        out = acc[at, :] + fresh[at, :] * values[:, g * HD : (g + 1) * HD]
        att_ref[:, h * HD : (h + 1) * HD] = out.astype(BF16)

    for copy in out_copies + ret_copies + [half_copy, shr_copy]:
        copy.wait_send()


def body(
    features, value_matrix, adapter_down, adapter_up, queries, new_key_rows, stored_key_cache,
    stored_value_cache, cache_length, resident_adapter_index, panel_owner_slot, outgoing_rows,
    outgoing_counts,
):
    replicas = lax.axis_size("replica")
    rows, width = features.shape
    half = resident_adapter_index.shape[0]
    cols = adapter_up.shape[2]
    heads = queries.shape[1] // HD
    ctx = stored_key_cache.shape[1]
    per_pair = max(2, -(-half // replicas))
    pieces = 16 // math.gcd(16, per_pair)
    sent = replicas * per_pair
    block = PANEL_SLOTS * RANKS
    anywhere = pl.BlockSpec(memory_space=pl.ANY)
    scalars = pl.BlockSpec(memory_space=pltpu.SMEM)
    vmem = pl.BlockSpec(memory_space=pltpu.VMEM)
    big = [features, value_matrix, adapter_down, adapter_up, queries, new_key_rows,
           stored_key_cache, stored_value_cache]
    dma = pltpu.SemaphoreType.DMA
    chunk = (replicas, per_pair * pieces, width // pieces)
    return pl.pallas_call(
        functools.partial(kernel, replicas, per_pair, pieces),
        out_shape=(
            jax.ShapeDtypeStruct((rows, cols), BF16),
            jax.ShapeDtypeStruct(queries.shape, BF16),
        ),
        in_specs=[anywhere] * 8 + [scalars] * 5,
        out_specs=(vmem, vmem),
        scratch_shapes=[pltpu.VMEM(a.shape, BF16) for a in big] + [
            pltpu.VMEM((width // pieces // HD, sent * pieces, HD), F32),
            pltpu.VMEM(chunk, BF16),
            pltpu.VMEM(chunk, BF16),
            pltpu.VMEM((2, rows + half, cols), F32),
            pltpu.VMEM((rows + half, cols), F32),
            pltpu.VMEM((sent, HD), F32),
            pltpu.VMEM((sent, HD), F32),
            pltpu.VMEM((replicas, block, cols), F32),
            pltpu.VMEM((replicas, block, cols), F32),
            pltpu.VMEM((rows * heads, HD), F32),
            pltpu.VMEM((rows * heads, HD), F32),
            pltpu.VMEM((rows, heads, ctx), F32),
            pltpu.VMEM((rows, heads, ctx), BF16),
            pltpu.VMEM((rows * heads, HD), F32),
            pltpu.VMEM((rows * heads, HD), F32),
            dma((5,)), dma((CHUNKS,)), dma((CHUNKS,)), dma((CHUNKS,)),
            dma((replicas,)), dma((replicas,)), dma((replicas,)), dma((replicas,)), dma((4,)),
        ],
        compiler_params=pltpu.CompilerParams(
            collective_id=0, has_side_effects=True, vmem_limit_bytes=48 * 1024 * 1024
        ),
        cost_estimate=pl.CostEstimate(
            flops=500_000_000, bytes_accessed=12_000_000, transcendentals=100_000
        ),
    )(*big, cache_length, resident_adapter_index, panel_owner_slot, outgoing_rows, outgoing_counts)


def solution(mesh):
    in_specs = (
        P(("groups", "replica"), "tensor"),
        P("tensor", None),
        P("replica", None, "tensor"),
        P("replica", None, "tensor"),
        P(("groups", "replica"), "tensor"),
        P(("groups", "replica"), "tensor"),
        P(("groups", "replica"), None, "tensor"),
        P(("groups", "replica"), None, "tensor"),
        P(("groups", "replica")),
        P(("groups", "replica")),
        P(("groups", "replica")),
        P(("groups", "replica"), None, None),
        P(("groups", "replica"), None),
    )
    out_specs = (P(("groups", "replica"), "tensor"), P(("groups", "replica"), "tensor"))
    return jax.shard_map(body, mesh=mesh, in_specs=in_specs, out_specs=out_specs, check_vma=False)
```

time: 118 us -> 31.5 us (0.27)
  matrix products: 25.1 us -> 0 us
  local copies, waits for them, and re-layouts: 34.8 us -> 11 us
  Pallas kernels: 0 us -> 19.4 us
  waiting for transfers between devices: 17 us -> 0 us
  between operations: 14.2 us -> 0.65 us
  starting transfers between devices: 13.3 us -> 0 us
  other arithmetic: 9.67 us -> 0 us
  blocking collectives: 2.59 us -> 0 us
    dot_general x12 -> x0, matrix products: 25.1 us -> none  [the longest x1 3.66 us: body(): jnp.dot(features, value_matrix, preferred_element_type=jnp.float32)]
    pallas_call x0 -> x1, Pallas kernels: none -> 19.4 us  [body(): pl.pallas_call(functools.partial(kernel, replicas, per_pair, pieces), out...]
    all_to_all x2 -> x0, waiting for transfers between devices: 16.9 us -> none  [the longest x1 16.9 us: body(): lax.all_to_all(down_send, 'replica', split_axis=0, concat_axis=0, tiled=T...]
    reshape x6 -> x0, local copies, waits for them, and re-layouts: 14 us -> none  [the longest x1 6.36 us: body(): received_down.reshape(panel_count * adapter_rank_size, half_width)]
    all_to_all x2 -> x0, starting transfers between devices: 13.3 us -> none  [the longest x1 7.28 us: body(): lax.all_to_all(up_send, 'replica', split_axis=0, concat_axis=0, tiled=True)]
    unnamed x16 -> x23, local copies, waits for them, and re-layouts: 2.32 us -> 11 us
    dot_general x4 -> x0, local copies, waits for them, and re-layouts: 5.73 us -> none  [the longest x1 3.46 us: body(): jnp.dot(selector, down_panels, preferred_element_type=jnp.bfloat16)]
    convert_element_type x3 -> x0, local copies, waits for them, and re-layouts: 3.45 us -> none  [the longest x1 1.4 us: attend(): fresh_weights.astype(jnp.float32)[..., None]]
  transfers between devices with their start and end apart: 3 -> 0, of which waited for: 1 -> 0; matrix products, arithmetic and copies ran while one was open for 51% -> 0% of each run, Pallas kernels for 0% -> 0%
where the time goes in v1:
time: 31.5 us; the launch traced here: 31.1 us
  Pallas kernels  19.4 us (62%)
  local copies, waits for them, and re-layouts  11 us (35%)
  between operations  0.65 us (2%)
    pallas_call x1, Pallas kernels, body(): pl.pallas_call(functools.partial(kernel, replicas, per_pair, pieces), out...  19.4 us
    unnamed x23, local copies, waits for them, and re-layouts  11 us

profile of v1, /device:TPU:0, one launch (start us, length us, event | category | flops | bytes accessed | tf_op | source)
XLA Modules:
  0.0 31.1 jit_solution(16912551796295071602)
XLA Ops:
  0.6 0.8 %copy.15.rows_ref = s32[1,8,2]{2,1,0:T(8,128)S(1)} copy(s32[1,8,2]{1,2,0:T(2,128)} %param.24) | data formatting | bytes 128 | tf_op args[11]
  1.4 0.0 copy-start
  1.4 1.9 %copy-done = bf16[48,128,256]{2,1,0:T(8,128)(2,1)S(1)} copy-done((bf16[48,128,256]{2,1,0:T(8,128)(2,1)S(1)}, bf16[48,128,256]{2,1,0:T(8,128)(2,1)}, u32[]{:S(2)}) %copy-start) | copy-done | bytes 3145752
  3.3 0.0 copy-start.1
  3.3 1.0 %copy-done.1 = bf16[4,16,4096]{2,1,0:T(8,128)(2,1)S(1)} copy-done((bf16[4,16,4096]{2,1,0:T(8,128)(2,1)S(1)}, bf16[4,16,4096]{2,1,0:T(8,128)(2,1)}, u32[]{:S(2)}) %copy-start.1) | copy-done | bytes 524312
  4.3 0.0 copy-start.2
  4.3 1.0 %copy-done.2 = bf16[48,4096]{1,0:T(8,128)(2,1)S(1)} copy-done((bf16[48,4096]{1,0:T(8,128)(2,1)S(1)}, bf16[48,4096]{1,0:T(8,128)(2,1)}, u32[]{:S(2)}) %copy-start.2) | copy-done | bytes 393240
  5.3 0.0 copy-start.3
  5.3 0.9 %copy-done.3 = bf16[48,2048]{1,0:T(8,128)(2,1)S(1)} copy-done((bf16[48,2048]{1,0:T(8,128)(2,1)S(1)}, bf16[48,2048]{1,0:T(8,128)(2,1)}, u32[]{:S(2)}) %copy-start.3) | copy-done | bytes 196632
  6.2 0.0 copy-start.4
  6.2 0.8 %copy-done.4 = bf16[4,16,256]{2,1,0:T(8,128)(2,1)S(1)} copy-done((bf16[4,16,256]{2,1,0:T(8,128)(2,1)S(1)}, bf16[4,16,256]{2,1,0:T(8,128)(2,1)}, u32[]{:S(2)}) %copy-start.4) | copy-done | bytes 32792
  7.0 0.0 copy-start.5
  7.0 0.7 %copy-done.5 = bf16[48,256]{1,0:T(8,128)(2,1)S(1)} copy-done((bf16[48,256]{1,0:T(8,128)(2,1)S(1)}, bf16[48,256]{1,0:T(8,128)(2,1)}, u32[]{:S(2)}) %copy-start.5) | copy-done | bytes 24600
  7.7 0.0 copy-start.6
  7.7 0.7 %copy-done.6 = s32[48]{0:T(128)S(1)} copy-done((s32[48]{0:T(128)S(1)}, s32[48]{0:T(128)}, u32[]{:S(2)}) %copy-start.6) | copy-done | bytes 216
  8.4 0.0 copy-start.7
  8.4 0.7 %copy-done.7 = s32[24]{0:T(128)S(1)} copy-done((s32[24]{0:T(128)S(1)}, s32[24]{0:T(128)}, u32[]{:S(2)}) %copy-start.7) | copy-done | bytes 120
  9.0 0.0 copy-start.8
  9.0 0.7 %copy-done.8 = s32[24]{0:T(128)S(1)} copy-done((s32[24]{0:T(128)S(1)}, s32[24]{0:T(128)}, u32[]{:S(2)}) %copy-start.8) | copy-done | bytes 120
  9.7 0.0 copy-start.9
  9.7 0.7 %copy-done.9 = s32[1,8]{1,0:T(1,128)S(1)} copy-done((s32[1,8]{1,0:T(1,128)S(1)}, s32[1,8]{1,0:T(1,128)}, u32[]{:S(2)}) %copy-start.9) | copy-done | bytes 56
  10.4 19.4 %shard_map.140 = (bf16[48,256]{1,0:T(8,128)(2,1)S(1)}, bf16[48,2048]{1,0:T(8,128)(2,1)S(1)}) custom-call(bf16[48,4096]{1,0:T(8,128)(2,1)S(1)} %copy-done.2, bf16[4096,512]{1,0:T(8,128)(2,1)} %vm_hbm.1, bf16[4,16,4096]{2,1,0:T(8,128)(2,1)S(1)} %copy-done.1, bf16[4,16,256]{2,1,0:T(8,128)(2,1)S(1)} %copy-done.4, bf16[48,2048]{1,0:T(8,128)(2,1)S(1)} %copy-done.3, ...), custom_call_target="tpu_custom_call" | custom-call | flops 500000000 | bytes 12000000 | tf_op jit(solution)/shard_map/pallas_call | solution.py:307
  29.8 0.6 %copy.18 = bf16[48,256]{1,0:T(8,128)(2,1)} copy(bf16[48,256]{1,0:T(8,128)(2,1)S(1)} %get-tuple-element.4) | data formatting | bytes 49152
  30.4 0.7 %copy.19 = bf16[48,2048]{1,0:T(8,128)(2,1)} copy(bf16[48,2048]{1,0:T(8,128)(2,1)S(1)} %get-tuple-element.5) | data formatting | bytes 393216
Async XLA Ops:
  1.4 1.9 %copy-start = (bf16[48,128,256]{2,1,0:T(8,128)(2,1)S(1)}, bf16[48,128,256]{2,1,0:T(8,128)(2,1)}, u32[]{:S(2)}) copy-start(bf16[48,128,256]{2,1,0:T(8,128)(2,1)} %k_hbm.1) | copy-start | bytes 9437188
  3.3 1.0 %copy-start.1 = (bf16[4,16,4096]{2,1,0:T(8,128)(2,1)S(1)}, bf16[4,16,4096]{2,1,0:T(8,128)(2,1)}, u32[]{:S(2)}) copy-start(bf16[4,16,4096]{2,1,0:T(8,128)(2,1)} %down_hbm.1) | copy-start | bytes 1572868
  4.3 1.0 %copy-start.2 = (bf16[48,4096]{1,0:T(8,128)(2,1)S(1)}, bf16[48,4096]{1,0:T(8,128)(2,1)}, u32[]{:S(2)}) copy-start(bf16[48,4096]{1,0:T(8,128)(2,1)} %feat_hbm.1) | copy-start | bytes 1179652
  5.3 0.9 %copy-start.3 = (bf16[48,2048]{1,0:T(8,128)(2,1)S(1)}, bf16[48,2048]{1,0:T(8,128)(2,1)}, u32[]{:S(2)}) copy-start(bf16[48,2048]{1,0:T(8,128)(2,1)} %q_hbm.1) | copy-start | bytes 589828
  6.2 0.8 %copy-start.4 = (bf16[4,16,256]{2,1,0:T(8,128)(2,1)S(1)}, bf16[4,16,256]{2,1,0:T(8,128)(2,1)}, u32[]{:S(2)}) copy-start(bf16[4,16,256]{2,1,0:T(8,128)(2,1)} %up_hbm.1) | copy-start | bytes 98308
  7.0 0.7 %copy-start.5 = (bf16[48,256]{1,0:T(8,128)(2,1)S(1)}, bf16[48,256]{1,0:T(8,128)(2,1)}, u32[]{:S(2)}) copy-start(bf16[48,256]{1,0:T(8,128)(2,1)} %nk_hbm.1) | copy-start | bytes 73732
  7.7 0.7 %copy-start.6 = (s32[48]{0:T(128)S(1)}, s32[48]{0:T(128)}, u32[]{:S(2)}) copy-start(s32[48]{0:T(128)} %len_ref.1) | copy-start | bytes 580
  8.4 0.7 %copy-start.7 = (s32[24]{0:T(128)S(1)}, s32[24]{0:T(128)}, u32[]{:S(2)}) copy-start(s32[24]{0:T(128)} %res_ref.1) | copy-start | bytes 292
  9.0 0.7 %copy-start.8 = (s32[24]{0:T(128)S(1)}, s32[24]{0:T(128)}, u32[]{:S(2)}) copy-start(s32[24]{0:T(128)} %slot_ref.1) | copy-start | bytes 292
  9.7 0.7 %copy-start.9 = (s32[1,8]{1,0:T(1,128)S(1)}, s32[1,8]{1,0:T(1,128)}, u32[]{:S(2)}) copy-start(s32[1,8]{1,0:T(1,128)} %count_ref.1) | copy-start | bytes 100

commit v2 on v1

--- a/solution.py
+++ b/solution.py
@@ -219,7 +219,7 @@
     for i in range(replicas):
         for s in range(PANEL_SLOTS):
             at = (sub // RANKS) == i * PANEL_SLOTS + s
-            value = jnp.where(s < count_ref[0, i], rows_ref[0, i, s], -1)
+            value = jnp.where(s < count_ref[0, i], rows_ref[0, s, i], -1)
             adapter = jnp.where(at, value, adapter)
     shape = (replicas * block, sent)
     sub_e, lane_e = iota(shape, 0), iota(shape, 1)
@@ -332,12 +332,13 @@
             dma((replicas,)), dma((replicas,)), dma((replicas,)), dma((replicas,)), dma((4,)),
         ],
         compiler_params=pltpu.CompilerParams(
-            collective_id=0, has_side_effects=True, vmem_limit_bytes=48 * 1024 * 1024
+            collective_id=0, has_side_effects=True, vmem_limit_bytes=63 * 1024 * 1024
         ),
         cost_estimate=pl.CostEstimate(
             flops=500_000_000, bytes_accessed=12_000_000, transcendentals=100_000
         ),
-    )(*big, cache_length, resident_adapter_index, panel_owner_slot, outgoing_rows, outgoing_counts)
+    )(*big, cache_length, resident_adapter_index, panel_owner_slot,
+      jnp.swapaxes(outgoing_rows, 1, 2), outgoing_counts)
 
 
 def solution(mesh):

time: 31.5 us -> 23.3 us (0.74)
  local copies, waits for them, and re-layouts: 11 us -> 2.96 us
    unnamed x23 -> x2, local copies, waits for them, and re-layouts: 11 us -> 2.96 us
where the time goes in v2:
time: 23.3 us; the launch traced here: 23.1 us
  Pallas kernels  19.5 us (84%)
  local copies, waits for them, and re-layouts  2.96 us (13%)
  between operations  0.64 us (3%)
    pallas_call x1, Pallas kernels, body(): pl.pallas_call(functools.partial(kernel, replicas, per_pair, pieces), out...  19.5 us
    unnamed x2, local copies, waits for them, and re-layouts  2.96 us

profile of v2, /device:TPU:0, one launch (start us, length us, event | category | flops | bytes accessed | tf_op | source)
XLA Modules:
  0.0 23.1 jit_solution(14984672883641801069)
XLA Ops:
  0.6 19.5 %shard_map.140 = (bf16[48,256]{1,0:T(8,128)(2,1)}, bf16[48,2048]{1,0:T(8,128)(2,1)}) custom-call(bf16[48,4096]{1,0:T(8,128)(2,1)} %feat_hbm.1, bf16[4096,512]{1,0:T(8,128)(2,1)} %vm_hbm.1, bf16[4,16,4096]{2,1,0:T(8,128)(2,1)} %down_hbm.1, bf16[4,16,256]{2,1,0:T(8,128)(2,1)} %up_hbm.1, bf16[48,2048]{1,0:T(8,128)(2,1)} %q_hbm.1, bf16[48,256]{1,0:T(8,128)(2,1)} %nk_hbm.1, ...), custom_call_target="tpu_custom_call" | custom-call | flops 500000000 | bytes 12000000 | tf_op jit(solution)/shard_map/pallas_call | solution.py:307
  20.1 1.3 %copy.17 = bf16[48,256]{1,0:T(8,128)(2,1)} copy(bf16[48,256]{1,0:T(8,128)(2,1)} %get-tuple-element.4) | data formatting | bytes 49152
  21.4 1.6 %copy.18 = bf16[48,2048]{1,0:T(8,128)(2,1)} copy(bf16[48,2048]{1,0:T(8,128)(2,1)} %get-tuple-element.5) | data formatting | bytes 393216

commit v3 on v2

--- a/solution.py
+++ b/solution.py
@@ -42,11 +42,12 @@
 def kernel(
     replicas, per_pair, pieces,
     feat_hbm, vm_hbm, down_hbm, up_hbm, q_hbm, nk_hbm, k_hbm, v_hbm,
-    len_ref, res_ref, slot_ref, rows_ref, count_ref,
+    len_hbm, res_hbm, slot_hbm, rows_hbm, count_hbm,
     nv_ref, att_ref,
     feat, vm, down, up, q, nk, kc, vc,
     x32, tx, rx, half_tx, half_rx, shr_tx, shr_rx, ret_tx, ret_rx,
     q3, nk3, sc, wt, fresh, acc,
+    len_ref, res_ref, slot_ref, rows_ref, count_ref,
     in_sem, vm_sem, k_sem, v_sem, tx_sem, rx_sem, ret_tx_sem, ret_rx_sem, peer_sem,
 ):
     me = lax.axis_index("replica")
@@ -66,11 +67,19 @@
     step = rows // CHUNKS
     depth = width // CHUNKS
 
+    barrier = pltpu.get_barrier_semaphore()
+    for d in range(1, replicas):
+        pl.semaphore_signal(
+            barrier, inc=1, device_id={"replica": lax.rem(me + d, replicas)}, device_id_type=MESH
+        )
+    pl.semaphore_signal(barrier, inc=1, device_id={"tensor": 1 - core}, device_id_type=MESH)
+
     def load(src, dst, sem):
         copy = pltpu.make_async_copy(src, dst, sem)
         copy.start()
         return copy
 
+    slot_in = load(slot_hbm, slot_ref, in_sem.at[5])
     feat_in = load(feat_hbm, feat, in_sem.at[0])
     down_in = load(down_hbm, down, in_sem.at[1])
     vm_in = [
@@ -84,29 +93,28 @@
         for c in range(CHUNKS)
     ]
     up_in = load(up_hbm, up, in_sem.at[4])
+    res_in = load(res_hbm, res_ref, in_sem.at[6])
+    len_in = load(len_hbm, len_ref, in_sem.at[7])
+    rows_in = load(rows_hbm, rows_ref, in_sem.at[8])
+    count_in = load(count_hbm, count_ref, in_sem.at[9])
     v_in = [
         load(v_hbm.at[pl.ds(c * step, step)], vc.at[pl.ds(c * step, step)], v_sem.at[c])
         for c in range(CHUNKS)
     ]
 
-    barrier = pltpu.get_barrier_semaphore()
-    for d in range(1, replicas):
-        pl.semaphore_signal(
-            barrier, inc=1, device_id={"replica": lax.rem(me + d, replicas)}, device_id_type=MESH
-        )
-    pl.semaphore_signal(barrier, inc=1, device_id={"tensor": 1 - core}, device_id_type=MESH)
-
     square = (rows, rows)
     sub, lane = iota(square, 0), iota(square, 1)
-    slot_l = spread(slot_ref, half, square, 1, half)
-    slot_s = spread(slot_ref, half, square, 0, half)
+    slot_in.wait()
+    slot_l = spread(slot_ref, half, (1, rows), 1, half)
+    slot_s = jnp.sum(jnp.where(sub == lane, slot_l, 0).astype(F32), axis=1, keepdims=True)
+    slot_s = slot_s.astype(I32)
     own_l, own_s = slot_l >> 1, slot_s >> 1
     same = own_l == own_s
     number_l = jnp.sum(jnp.where(same & (sub < lane), 1.0, 0.0), axis=0, keepdims=True).astype(I32)
     number_s = jnp.sum(jnp.where(same & (lane < sub), 1.0, 0.0), axis=1, keepdims=True).astype(I32)
-    goes = jnp.where(lane[:1] >= half, own_l[:1] * per_pair + number_l, -1)
+    goes = jnp.where(lane[:1] >= half, own_l * per_pair + number_l, -1)
     chooser = jnp.where(iota((sent, rows), 0) == goes, 1.0, 0.0).astype(BF16)
-    comes = own_s[:, :1] * block + (slot_s[:, :1] & 1) * RANKS + number_s
+    comes = own_s * block + (slot_s & 1) * RANKS + number_s
     comes = jnp.where(sub[:, :1] >= half, comes, -1)
     picker = jnp.where(iota((rows, replicas * block), 1) == comes, 1.0, 0.0).astype(BF16)
 
@@ -122,7 +130,8 @@
 
     pl.semaphore_wait(barrier, replicas)
     out_copies = []
-    for d in range(1, replicas):
+    order = sorted(range(1, replicas), key=lambda d: -abs(2 * d - replicas))
+    for d in order:
         there = lax.rem(me + d, replicas)
         copy = pltpu.make_async_remote_copy(
             src_ref=tx.at[there], dst_ref=rx.at[me],
@@ -135,6 +144,7 @@
 
     down_in.wait()
     shrunk = dot(feat[...], down[...].reshape(flat, width), NT)
+    res_in.wait()
     res_s = spread(res_ref, half, (rows, flat), 0, 0)
     shrunk = jnp.where((iota((rows, flat), 1) // rank) == res_s, shrunk, 0.0)[:half]
     base = jnp.zeros((rows, 2 * cols), F32)
@@ -158,6 +168,7 @@
         g = h // group
         q3[pl.ds(h, rows, stride=heads), :] = q[:, h * HD : (h + 1) * HD].astype(F32)
         nk3[pl.ds(h, rows, stride=heads), :] = nk[:, g * HD : (g + 1) * HD].astype(F32)
+    len_in.wait()
     scale = 1.0 / math.sqrt(HD)
     head_of = iota((heads, HD), 0) // group
     place = iota((heads, ctx), 1)
@@ -213,6 +224,8 @@
         soften(c)
 
     up_in.wait()
+    rows_in.wait()
+    count_in.wait()
     shape = (replicas * block, flat)
     sub, lane = iota(shape, 0), iota(shape, 1)
     adapter = jnp.full(shape, -1, I32)
@@ -234,7 +247,7 @@
     low = jnp.where(keep, dot(expand, low), 0.0).astype(BF16)
     ret_tx[...] = (dot(high, up_flat) + dot(low, up_flat)).reshape(ret_tx.shape)
     ret_copies = []
-    for d in range(1, replicas):
+    for d in order:
         there = lax.rem(me + d, replicas)
         copy = pltpu.make_async_remote_copy(
             src_ref=ret_tx.at[there], dst_ref=ret_rx.at[me],
@@ -282,6 +295,11 @@
         copy.wait_send()
 
 
+def hand_over(nv_in, att_in, nv_out, att_out):
+    nv_out[...] = nv_in[...]
+    att_out[...] = att_in[...]
+
+
 def body(
     features, value_matrix, adapter_down, adapter_up, queries, new_key_rows, stored_key_cache,
     stored_value_cache, cache_length, resident_adapter_index, panel_owner_slot, outgoing_rows,
@@ -298,19 +316,20 @@
     sent = replicas * per_pair
     block = PANEL_SLOTS * RANKS
     anywhere = pl.BlockSpec(memory_space=pl.ANY)
-    scalars = pl.BlockSpec(memory_space=pltpu.SMEM)
     vmem = pl.BlockSpec(memory_space=pltpu.VMEM)
     big = [features, value_matrix, adapter_down, adapter_up, queries, new_key_rows,
            stored_key_cache, stored_value_cache]
+    small = [cache_length, resident_adapter_index, panel_owner_slot,
+             jnp.swapaxes(outgoing_rows, 1, 2), outgoing_counts]
     dma = pltpu.SemaphoreType.DMA
     chunk = (replicas, per_pair * pieces, width // pieces)
-    return pl.pallas_call(
+    values, attended = pl.pallas_call(
         functools.partial(kernel, replicas, per_pair, pieces),
         out_shape=(
             jax.ShapeDtypeStruct((rows, cols), BF16),
             jax.ShapeDtypeStruct(queries.shape, BF16),
         ),
-        in_specs=[anywhere] * 8 + [scalars] * 5,
+        in_specs=[anywhere] * 13,
         out_specs=(vmem, vmem),
         scratch_shapes=[pltpu.VMEM(a.shape, BF16) for a in big] + [
             pltpu.VMEM((width // pieces // HD, sent * pieces, HD), F32),
@@ -328,7 +347,8 @@
             pltpu.VMEM((rows, heads, ctx), BF16),
             pltpu.VMEM((rows * heads, HD), F32),
             pltpu.VMEM((rows * heads, HD), F32),
-            dma((5,)), dma((CHUNKS,)), dma((CHUNKS,)), dma((CHUNKS,)),
+            *[pltpu.SMEM(a.shape, I32) for a in small],
+            dma((10,)), dma((CHUNKS,)), dma((CHUNKS,)), dma((CHUNKS,)),
             dma((replicas,)), dma((replicas,)), dma((replicas,)), dma((replicas,)), dma((4,)),
         ],
         compiler_params=pltpu.CompilerParams(
@@ -337,8 +357,17 @@
         cost_estimate=pl.CostEstimate(
             flops=500_000_000, bytes_accessed=12_000_000, transcendentals=100_000
         ),
-    )(*big, cache_length, resident_adapter_index, panel_owner_slot,
-      jnp.swapaxes(outgoing_rows, 1, 2), outgoing_counts)
+    )(*big, *small)
+    return pl.pallas_call(
+        hand_over,
+        out_shape=(
+            jax.ShapeDtypeStruct(values.shape, BF16),
+            jax.ShapeDtypeStruct(attended.shape, BF16),
+        ),
+        in_specs=[vmem] * 2,
+        out_specs=(vmem, vmem),
+
+    )(values, attended)
 
 
 def solution(mesh):

time: 23.3 us -> 20.5 us (0.88)
  local copies, waits for them, and re-layouts: 2.96 us -> 0 us
    unnamed x2 -> x0, local copies, waits for them, and re-layouts: 2.96 us -> none
    pallas_call x0 -> x1, Pallas kernels: none -> 1.64 us  [body(): pl.pallas_call(hand_over, out_shape=(jax.ShapeDtypeStruct(values.shape, B...]
    pallas_call x1, Pallas kernels: 19.5 us -> 18.1 us  [body(): pl.pallas_call(functools.partial(kernel, replicas, per_pair, pieces), out...]
where the time goes in v3:
time: 20.5 us; the launch traced here: 20.3 us
  Pallas kernels  19.7 us (96%)
  between operations  0.64 us (3%)
    pallas_call x1, Pallas kernels, body(): pl.pallas_call(functools.partial(kernel, replicas, per_pair, pieces), out...  18.1 us
    pallas_call x1, Pallas kernels, body(): pl.pallas_call(hand_over, out_shape=(jax.ShapeDtypeStruct(values.shape, B...  1.64 us

profile of v3, /device:TPU:0, one launch (start us, length us, event | category | flops | bytes accessed | tf_op | source)
XLA Modules:
  0.0 20.3 jit_solution(13813531612344376305)
XLA Ops:
  0.6 18.1 %shard_map.140 = (bf16[48,256]{1,0:T(8,128)(2,1)}, bf16[48,2048]{1,0:T(8,128)(2,1)}) custom-call(bf16[48,4096]{1,0:T(8,128)(2,1)} %feat_hbm.1, bf16[4096,512]{1,0:T(8,128)(2,1)} %vm_hbm.1, bf16[4,16,4096]{2,1,0:T(8,128)(2,1)} %down_hbm.1, bf16[4,16,256]{2,1,0:T(8,128)(2,1)} %up_hbm.1, bf16[48,2048]{1,0:T(8,128)(2,1)} %q_hbm.1, bf16[48,256]{1,0:T(8,128)(2,1)} %nk_hbm.1, ...), custom_call_target="tpu_custom_call" | custom-call | flops 500000000 | bytes 12000000 | tf_op jit(solution)/shard_map/pallas_call | solution.py:326
  18.7 1.6 %shard_map.141 = (bf16[48,256]{1,0:T(8,128)(2,1)}, bf16[48,2048]{1,0:T(8,128)(2,1)}) custom-call(bf16[48,256]{1,0:T(8,128)(2,1)} %get-tuple-element.4.nv_in, bf16[48,2048]{1,0:T(8,128)(2,1)} %get-tuple-element.5.att_in), custom_call_target="tpu_custom_call" | custom-call | tf_op jit(solution)/shard_map/pallas_call | solution.py:361

commit v4 on v3

--- a/solution.py
+++ b/solution.py
@@ -16,6 +16,7 @@
 NT = (((1,), (1,)), ((), ()))
 RANKS = 4
 CHUNKS = 4
+BATCHES = 2
 
 
 def iota(shape, axis):
@@ -102,6 +103,18 @@
         for c in range(CHUNKS)
     ]
 
+    order = [0] + sorted(range(1, replicas), key=lambda k: -abs(2 * k - replicas))
+
+    def partner(offset, sign):
+        return lax.rem(me + sign * offset + replicas, replicas)
+
+    def slot_of(owner):
+        offset = jnp.where(owner < me, owner - me + replicas, owner - me)
+        out = jnp.zeros_like(owner)
+        for k in range(1, replicas):
+            out = jnp.where(offset == order[k], k, out)
+        return out
+
     square = (rows, rows)
     sub, lane = iota(square, 0), iota(square, 1)
     slot_in.wait()
@@ -112,9 +125,9 @@
     same = own_l == own_s
     number_l = jnp.sum(jnp.where(same & (sub < lane), 1.0, 0.0), axis=0, keepdims=True).astype(I32)
     number_s = jnp.sum(jnp.where(same & (lane < sub), 1.0, 0.0), axis=1, keepdims=True).astype(I32)
-    goes = jnp.where(lane[:1] >= half, own_l * per_pair + number_l, -1)
+    goes = jnp.where(lane[:1] >= half, slot_of(own_l) * per_pair + number_l, -1)
     chooser = jnp.where(iota((sent, rows), 0) == goes, 1.0, 0.0).astype(BF16)
-    comes = own_s * block + (slot_s & 1) * RANKS + number_s
+    comes = slot_of(own_s) * block + (slot_s & 1) * RANKS + number_s
     comes = jnp.where(sub[:, :1] >= half, comes, -1)
     picker = jnp.where(iota((rows, replicas * block), 1) == comes, 1.0, 0.0).astype(BF16)
 
@@ -129,18 +142,16 @@
         tx[:, :, b * HD : (b + 1) * HD] = x32[b].astype(BF16).reshape(replicas, -1, HD)
 
     pl.semaphore_wait(barrier, replicas)
-    out_copies = []
-    order = sorted(range(1, replicas), key=lambda d: -abs(2 * d - replicas))
-    for d in order:
-        there = lax.rem(me + d, replicas)
+    out_copies = [None]
+    for k in range(1, replicas):
         copy = pltpu.make_async_remote_copy(
-            src_ref=tx.at[there], dst_ref=rx.at[me],
-            send_sem=tx_sem.at[d], recv_sem=rx_sem.at[d],
-            device_id={"replica": there}, device_id_type=MESH,
+            src_ref=tx.at[k], dst_ref=rx.at[k],
+            send_sem=tx_sem.at[k], recv_sem=rx_sem.at[k],
+            device_id={"replica": partner(order[k], 1)}, device_id_type=MESH,
         )
         copy.start()
         out_copies.append(copy)
-    rx[me] = tx[me]
+    rx[0] = tx[0]
 
     down_in.wait()
     shrunk = dot(feat[...], down[...].reshape(flat, width), NT)
@@ -190,23 +201,78 @@
             0, step // unroll, lambda i, _, c=c: score(c * step + i * unroll), None
         )
 
-    for copy in out_copies:
-        copy.wait_recv()
-    for b in range(lanes):
-        x32[b] = rx[:, :, b * HD : (b + 1) * HD].reshape(sent * pieces, HD).astype(F32)
-    foreign = jnp.zeros((sent, flat), F32)
-    for p in range(pieces):
-        x_p = [x32[b, pl.ds(p, sent, stride=pieces), :] for b in range(lanes)]
-        x_p = jnp.concatenate(x_p, axis=1).astype(BF16)
-        foreign += dot(x_p, down[:, :, p * piece : (p + 1) * piece].reshape(flat, piece), NT)
-    shr_tx[...] = jnp.concatenate([foreign, jnp.zeros((sent, HD - flat), F32)], axis=1)
-    shr_copy = pltpu.make_async_remote_copy(
-        src_ref=shr_tx, dst_ref=shr_rx,
-        send_sem=peer_sem.at[2], recv_sem=peer_sem.at[3],
-        device_id={"tensor": 1 - core}, device_id_type=MESH,
-    )
-    shr_copy.start()
-
+    batch = replicas // BATCHES
+    batch_rows = batch * per_pair
+    shr_tx[...] = jnp.zeros_like(shr_tx)
+
+    def shrink_batch(n):
+        mine = slice(n * batch, (n + 1) * batch)
+        for copy in out_copies[mine]:
+            if copy is not None:
+                copy.wait_recv()
+        first = n * batch_rows * pieces
+        for b in range(lanes):
+            x32[b, pl.ds(first, batch_rows * pieces), :] = (
+                rx[mine, :, b * HD : (b + 1) * HD].reshape(batch_rows * pieces, HD).astype(F32)
+            )
+        foreign = jnp.zeros((batch_rows, flat), F32)
+        for p in range(pieces):
+            x_p = [x32[b, pl.ds(first + p, batch_rows, stride=pieces), :] for b in range(lanes)]
+            x_p = jnp.concatenate(x_p, axis=1).astype(BF16)
+            foreign += dot(x_p, down[:, :, p * piece : (p + 1) * piece].reshape(flat, piece), NT)
+        shr_tx[n, :batch_rows, :flat] = foreign
+        copy = pltpu.make_async_remote_copy(
+            src_ref=shr_tx.at[n], dst_ref=shr_rx.at[n],
+            send_sem=peer_sem.at[2 + 2 * n], recv_sem=peer_sem.at[3 + 2 * n],
+            device_id={"tensor": 1 - core}, device_id_type=MESH,
+        )
+        copy.start()
+        return copy
+
+    shr_copies = [shrink_batch(0)]
+    for n in range(1, BATCHES):
+        shr_copies.append(shrink_batch(n))
+
+    up_in.wait()
+    rows_in.wait()
+    count_in.wait()
+    shape = (batch * block, batch_rows)
+    sub_e, lane_e = iota(shape, 0), iota(shape, 1)
+    place_e = sub_e & (RANKS - 1)
+    expand = ((sub_e // block) * per_pair + place_e == lane_e) & (place_e < per_pair)
+    expand = jnp.where(expand, 1.0, 0.0).astype(BF16)
+    up_flat = up[...].reshape(flat, cols)
+    ret_copies = [None]
+
+    def return_batch(n):
+        shape = (batch * block, flat)
+        sub, lane = iota(shape, 0), iota(shape, 1)
+        adapter = jnp.full(shape, -1, I32)
+        for i in range(batch):
+            source = partner(order[n * batch + i], -1)
+            for s in range(PANEL_SLOTS):
+                at = (sub // RANKS) == i * PANEL_SLOTS + s
+                value = jnp.where(s < count_ref[0, source], rows_ref[0, s, source], -1)
+                adapter = jnp.where(at, value, adapter)
+        keep = (lane // rank) == adapter
+        shr_copies[n].wait_recv()
+        high, low = split(shr_tx[n, :batch_rows, :flat] + shr_rx[n, :batch_rows, :flat])
+        high = jnp.where(keep, dot(expand, high), 0.0).astype(BF16)
+        low = jnp.where(keep, dot(expand, low), 0.0).astype(BF16)
+        delta = dot(high, up_flat) + dot(low, up_flat)
+        ret_tx[n * batch : (n + 1) * batch] = delta.reshape(batch, block, cols)
+        for k in range(max(1, n * batch), (n + 1) * batch):
+            copy = pltpu.make_async_remote_copy(
+                src_ref=ret_tx.at[k], dst_ref=ret_rx.at[k],
+                send_sem=ret_tx_sem.at[k], recv_sem=ret_rx_sem.at[k],
+                device_id={"replica": partner(order[k], -1)}, device_id_type=MESH,
+            )
+            copy.start()
+            ret_copies.append(copy)
+
+    for n in range(BATCHES):
+        return_batch(n)
+    ret_rx[0] = ret_tx[0]
     def soften(c):
         r = pl.ds(c * step, step)
         flat_r = pl.ds(c * step * heads, step * heads)
@@ -223,41 +289,6 @@
     for c in range(CHUNKS):
         soften(c)
 
-    up_in.wait()
-    rows_in.wait()
-    count_in.wait()
-    shape = (replicas * block, flat)
-    sub, lane = iota(shape, 0), iota(shape, 1)
-    adapter = jnp.full(shape, -1, I32)
-    for i in range(replicas):
-        for s in range(PANEL_SLOTS):
-            at = (sub // RANKS) == i * PANEL_SLOTS + s
-            value = jnp.where(s < count_ref[0, i], rows_ref[0, s, i], -1)
-            adapter = jnp.where(at, value, adapter)
-    shape = (replicas * block, sent)
-    sub_e, lane_e = iota(shape, 0), iota(shape, 1)
-    place_e = sub_e & (RANKS - 1)
-    expand = ((sub_e // block) * per_pair + place_e == lane_e) & (place_e < per_pair)
-    expand = jnp.where(expand, 1.0, 0.0).astype(BF16)
-    up_flat = up[...].reshape(flat, cols)
-    shr_copy.wait_recv()
-    high, low = split(shr_tx[:, :flat] + shr_rx[:, :flat])
-    keep = (lane // rank) == adapter
-    high = jnp.where(keep, dot(expand, high), 0.0).astype(BF16)
-    low = jnp.where(keep, dot(expand, low), 0.0).astype(BF16)
-    ret_tx[...] = (dot(high, up_flat) + dot(low, up_flat)).reshape(ret_tx.shape)
-    ret_copies = []
-    for d in order:
-        there = lax.rem(me + d, replicas)
-        copy = pltpu.make_async_remote_copy(
-            src_ref=ret_tx.at[there], dst_ref=ret_rx.at[me],
-            send_sem=ret_tx_sem.at[d], recv_sem=ret_rx_sem.at[d],
-            device_id={"replica": there}, device_id_type=MESH,
-        )
-        copy.start()
-        ret_copies.append(copy)
-    ret_rx[me] = ret_tx[me]
-
     def gather(base_row):
         for u in range(unroll):
             r = base_row + u
@@ -278,7 +309,7 @@
     high, low = split(both[rows:, :flat])
     resident = dot(high, up_flat) + dot(low, up_flat)
     resident = jnp.concatenate([resident, jnp.zeros((rows - half, cols), F32)], axis=0)
-    for copy in ret_copies:
+    for copy in ret_copies[1:]:
         copy.wait_recv()
     high, low = split(ret_rx[...].reshape(replicas * block, cols))
     adapted = resident + (dot(picker, high) + dot(picker, low))
@@ -291,13 +322,8 @@
         out = acc[at, :] + fresh[at, :] * values[:, g * HD : (g + 1) * HD]
         att_ref[:, h * HD : (h + 1) * HD] = out.astype(BF16)
 
-    for copy in out_copies + ret_copies + [half_copy, shr_copy]:
+    for copy in out_copies[1:] + ret_copies[1:] + shr_copies + [half_copy]:
         copy.wait_send()
-
-
-def hand_over(nv_in, att_in, nv_out, att_out):
-    nv_out[...] = nv_in[...]
-    att_out[...] = att_in[...]
 
 
 def body(
@@ -323,7 +349,7 @@
              jnp.swapaxes(outgoing_rows, 1, 2), outgoing_counts]
     dma = pltpu.SemaphoreType.DMA
     chunk = (replicas, per_pair * pieces, width // pieces)
-    values, attended = pl.pallas_call(
+    return pl.pallas_call(
         functools.partial(kernel, replicas, per_pair, pieces),
         out_shape=(
             jax.ShapeDtypeStruct((rows, cols), BF16),
@@ -337,8 +363,8 @@
             pltpu.VMEM(chunk, BF16),
             pltpu.VMEM((2, rows + half, cols), F32),
             pltpu.VMEM((rows + half, cols), F32),
-            pltpu.VMEM((sent, HD), F32),
-            pltpu.VMEM((sent, HD), F32),
+            pltpu.VMEM((BATCHES, -(-sent // BATCHES // 8) * 8, HD), F32),
+            pltpu.VMEM((BATCHES, -(-sent // BATCHES // 8) * 8, HD), F32),
             pltpu.VMEM((replicas, block, cols), F32),
             pltpu.VMEM((replicas, block, cols), F32),
             pltpu.VMEM((rows * heads, HD), F32),
@@ -349,25 +375,15 @@
             pltpu.VMEM((rows * heads, HD), F32),
             *[pltpu.SMEM(a.shape, I32) for a in small],
             dma((10,)), dma((CHUNKS,)), dma((CHUNKS,)), dma((CHUNKS,)),
-            dma((replicas,)), dma((replicas,)), dma((replicas,)), dma((replicas,)), dma((4,)),
+            dma((replicas,)), dma((replicas,)), dma((replicas,)), dma((replicas,)), dma((2 + 2 * BATCHES,)),
         ],
         compiler_params=pltpu.CompilerParams(
-            collective_id=0, has_side_effects=True, vmem_limit_bytes=63 * 1024 * 1024
+            collective_id=0, has_side_effects=True, vmem_limit_bytes=40 * 1024 * 1024
         ),
         cost_estimate=pl.CostEstimate(
             flops=500_000_000, bytes_accessed=12_000_000, transcendentals=100_000
         ),
-    )(*big, *small)
-    return pl.pallas_call(
-        hand_over,
-        out_shape=(
-            jax.ShapeDtypeStruct(values.shape, BF16),
-            jax.ShapeDtypeStruct(attended.shape, BF16),
-        ),
-        in_specs=[vmem] * 2,
-        out_specs=(vmem, vmem),
-
-    )(values, attended)
+    )(*[pltpu.with_memory_space_constraint(a, pltpu.HBM) for a in big + small])
 
 
 def solution(mesh):

time: 20.5 us -> 19.1 us (0.932)
  Pallas kernels: 19.7 us -> 17.1 us
  local copies, waits for them, and re-layouts: 0 us -> 1.29 us
    pallas_call x1 -> x0, Pallas kernels: 1.64 us -> none  [body(): pl.pallas_call(hand_over, out_shape=(jax.ShapeDtypeStruct(values.shape, B...]
    unnamed x0 -> x2, local copies, waits for them, and re-layouts: none -> 1.29 us
    pallas_call x1, Pallas kernels: 18.1 us -> 17.1 us  [body(): pl.pallas_call(functools.partial(kernel, replicas, per_pair, pieces), out...]
where the time goes in v4:
time: 19.1 us; the launch traced here: 19 us
  Pallas kernels  17.1 us (90%)
  local copies, waits for them, and re-layouts  1.29 us (7%)
  between operations  0.64 us (3%)
    pallas_call x1, Pallas kernels, body(): pl.pallas_call(functools.partial(kernel, replicas, per_pair, pieces), out...  17.1 us
    unnamed x2, local copies, waits for them, and re-layouts  1.29 us

profile of v4, /device:TPU:0, one launch (start us, length us, event | category | flops | bytes accessed | tf_op | source)
XLA Modules:
  0.0 19.0 jit_solution(12081238796447094082)
XLA Ops:
  0.6 17.1 %shard_map.140 = (bf16[48,256]{1,0:T(8,128)(2,1)S(1)}, bf16[48,2048]{1,0:T(8,128)(2,1)S(1)}) custom-call(bf16[48,4096]{1,0:T(8,128)(2,1)} %feat_hbm.1, bf16[4096,512]{1,0:T(8,128)(2,1)} %vm_hbm.1, bf16[4,16,4096]{2,1,0:T(8,128)(2,1)} %down_hbm.1, bf16[4,16,256]{2,1,0:T(8,128)(2,1)} %up_hbm.1, bf16[48,2048]{1,0:T(8,128)(2,1)} %q_hbm.1, ...), custom_call_target="tpu_custom_call" | custom-call | flops 500000000 | bytes 12000000 | tf_op jit(solution)/shard_map/pallas_call | solution.py:352
  17.7 0.6 %copy.17 = bf16[48,256]{1,0:T(8,128)(2,1)} copy(bf16[48,256]{1,0:T(8,128)(2,1)S(1)} %get-tuple-element.4) | data formatting | bytes 49152
  18.3 0.7 %copy.18 = bf16[48,2048]{1,0:T(8,128)(2,1)} copy(bf16[48,2048]{1,0:T(8,128)(2,1)S(1)} %get-tuple-element.5) | data formatting | bytes 393216

commit v5 on v4

--- a/solution.py
+++ b/solution.py
@@ -15,7 +15,7 @@
 F32, BF16, I32 = jnp.float32, jnp.bfloat16, jnp.int32
 NT = (((1,), (1,)), ((), ()))
 RANKS = 4
-CHUNKS = 4
+CHUNKS = 2
 BATCHES = 2
 
 

time: 19.1 us -> 19.1 us (level)
  no operation moved by 1% of the time
where the time goes in v5:
time: 19.1 us; the launch traced here: 18.9 us
  Pallas kernels  17 us (89%)
  local copies, waits for them, and re-layouts  1.29 us (7%)
  between operations  0.64 us (3%)
    pallas_call x1, Pallas kernels, body(): pl.pallas_call(functools.partial(kernel, replicas, per_pair, pieces), out...  17 us
    unnamed x2, local copies, waits for them, and re-layouts  1.29 us

profile of v5, /device:TPU:0, one launch (start us, length us, event | category | flops | bytes accessed | tf_op | source)
XLA Modules:
  0.0 18.9 jit_solution(12159855299002480779)
XLA Ops:
  0.6 17.0 %shard_map.140 = (bf16[48,256]{1,0:T(8,128)(2,1)S(1)}, bf16[48,2048]{1,0:T(8,128)(2,1)S(1)}) custom-call(bf16[48,4096]{1,0:T(8,128)(2,1)} %feat_hbm.1, bf16[4096,512]{1,0:T(8,128)(2,1)} %vm_hbm.1, bf16[4,16,4096]{2,1,0:T(8,128)(2,1)} %down_hbm.1, bf16[4,16,256]{2,1,0:T(8,128)(2,1)} %up_hbm.1, bf16[48,2048]{1,0:T(8,128)(2,1)} %q_hbm.1, ...), custom_call_target="tpu_custom_call" | custom-call | flops 500000000 | bytes 12000000 | tf_op jit(solution)/shard_map/pallas_call | solution.py:352
  17.6 0.6 %copy.17 = bf16[48,256]{1,0:T(8,128)(2,1)} copy(bf16[48,256]{1,0:T(8,128)(2,1)S(1)} %get-tuple-element.4) | data formatting | bytes 49152
  18.3 0.7 %copy.18 = bf16[48,2048]{1,0:T(8,128)(2,1)} copy(bf16[48,2048]{1,0:T(8,128)(2,1)S(1)} %get-tuple-element.5) | data formatting | bytes 393216
